TPU v7x, 1024 devices: a whole 8x8x8 slice. The times are simulated.
1024 devices in a mesh: dp: 64 (over z, y), head: 16 (over x, core).
Axes of the slice: x: 8, y: 8, z: 8, core: 2. Of those that a mesh axis runs over, the one named last changes fastest.
Arguments:
- latent: bfloat16 [98304, 512], P('dp', 'head'), may hold values from -16 to 16
- value_grad: bfloat16 [98304, 8192], P('dp', 'head'), may hold values from -6 to 6
- lengths: int32 [64], replicated, may hold values from 1 to 1536, 32768 in all
Outputs:
- update: bfloat16 [64, 512, 128], P('head')
Inputs may be any that keep to these rules, and one draw needn't show every extreme that they name: The lengths sum to 32768; the longest is exactly 1536.
All inputs are finite; a program needn't handle non-finite values.
Results may differ from a plain program's by a relative error of at most 0.035.
Values may be sent and summed in bfloat16 or wider, within the bound.
No kernel may reach another device: no remote copies, remote signals or barrier semaphores. Data moves between devices by JAX's collectives and lax.ppermute only.
A program may use at most 32 MiB of HBM per device.

v0:
```python
import jax
import jax.numpy as jnp
from jax import lax
from jax.sharding import PartitionSpec as P

KV_RANK = 512
V_DIM = 128
ITERS = 5


epsilon = 1e-07
coef_one = 3.4445
coef_two = -4.775
coef_three = 2.0315


def body(latent, value_grad, lengths):
    capacity, lat_cols = latent.shape
    grad_width = value_grad.shape[1]
    head_count = grad_width // V_DIM
    my_index = lax.axis_index("dp")
    own_length = lengths[my_index]
    slot_live = jnp.arange(capacity, dtype=jnp.int32) < own_length
    rows_grad = jnp.where(slot_live[:, None], value_grad, jnp.zeros_like(value_grad))
    partial_sum = lax.dot_general(
        lax.all_gather(latent, "head", axis=1, tiled=True),
        rows_grad,
        (((0,), (0,)), ((), ())),
        preferred_element_type=jnp.float32,
    )
    dw_shard = lax.psum_scatter(partial_sum, "dp", scatter_dimension=0, tiled=True)
    shard_heads = dw_shard.reshape(dw_shard.shape[0], head_count, V_DIM)
    local_squares = jnp.sum(shard_heads * shard_heads, axis=(0, 2))
    square_total = lax.psum(local_squares, "dp")
    head_norm = jnp.sqrt(square_total)
    ortho_shard = (shard_heads / (head_norm[None, :, None] + epsilon)).astype(jnp.bfloat16)
    ortho = lax.all_gather(ortho_shard, "dp", axis=0, tiled=True)
    for step in range(ITERS):
        gram_mat = jnp.einsum(
            "rhv,rhw->hvw", ortho, ortho, preferred_element_type=jnp.float32
        ).astype(jnp.bfloat16)
        squared = jnp.einsum("hvu,huw->hvw", gram_mat, gram_mat, preferred_element_type=jnp.float32)
        poly_mat = (coef_two * gram_mat.astype(jnp.float32) + coef_three * squared).astype(
            jnp.bfloat16
        )
        product = jnp.einsum("rhv,hvw->rhw", ortho, poly_mat, preferred_element_type=jnp.float32)
        ortho = (coef_one * ortho.astype(jnp.float32) + product).astype(jnp.bfloat16)
    scale = 0.2 * max(KV_RANK, V_DIM) ** 0.5
    update = (scale * ortho.astype(jnp.float32)).astype(jnp.bfloat16)
    return jnp.transpose(update, (1, 0, 2))


def solution(mesh):
    return jax.shard_map(
        body,
        mesh=mesh,
        in_specs=(P("dp", "head"), P("dp", "head"), P()),
        out_specs=P("head", None, None),
        check_vma=False,
    )
```

profile of v0, /device:TPU:16, one launch (start us, length us, event | category | flops | bytes accessed | tf_op | source)
XLA Modules:
  0.0 445.2 jit_solution(231183179342599252)
XLA Ops:
  6.5 0.0 all-gather.2.cloned.1.call-start
  6.5 0.7 all-gather.2.cloned.1.call-update
  7.3 0.0 all-reduce.3.cloned.1.call-start
  7.3 1.2 dynamic_slice.3
  8.5 0.7 iota_compare_fusion
  9.2 55.9 %all-gather.2.cloned.1.call-done = bf16[1536,512]{0,1:T(8,128)(2,1)} async-done(((bf16[1536,32]{0,1:T(8,128)(2,1)}), bf16[1536,512]{0,1:T(8,128)(2,1)}) %all-gather.2.cloned.1.call-update) | async-done | bytes 1572880 | tf_op jit(solution)/shard_map/all_gather | solution.py:26
  65.2 4.2 fusion.3
  69.3 0.0 all-reduce.3.cloned.1.call-update
  69.4 1.3 dynamic-slice
  71.3 171.6 %all-reduce.3.cloned.1.call-done = f32[512,512]{0,1:T(8,128)} async-done(((f32[512,512]{0,1:T(8,128)}), f32[512,512]{0,1:T(8,128)}) %all-reduce.3.cloned.1.call-update) | async-done | bytes 1048592
  242.9 1.2 multiply_reduce_fusion
  244.1 0.1 bitcast_reduce_fusion
  244.2 0.1 copy.48
  244.3 139.2 %psum.7 = f32[4]{0:T(128)S(1)} all-reduce(f32[4]{0:T(128)S(1)} %bitcast_reduce_fusion), channel_id=1, replica_groups=mesh['dp'=64,'head'=16] {'dp'}, use_global_device_ids=true, to_apply=%region_3.4 | all-reduce | flops 4 | bytes 32 | tf_op jit(solution)/shard_map/psum | solution.py:34
  383.5 0.1 fusion.51
  383.6 50.0 %all_gather.7 = bf16[512,4,128]{2,0,1:T(8,128)(2,1)S(1)} all-gather(bf16[8,4,128]{2,0,1:T(8,128)(2,1)S(1)} %fusion.51), channel_id=1, replica_groups=mesh['dp'=64,'head'=16] {'dp'}, dimensions={0}, use_global_device_ids=true | all-gather | bytes 532480 | tf_op jit(solution)/shard_map/all_gather | solution.py:37
  433.6 0.4 convolution_convert_fusion.4
  434.0 0.4 fusion.11
  434.4 0.3 convolution_convert_fusion.3
  434.8 0.4 fusion.12
  435.2 0.3 convolution_convert_fusion.2
  435.6 0.4 fusion.13
  436.0 0.3 convolution_convert_fusion.1
  436.3 0.4 fusion.14
  436.8 0.3 convolution_convert_fusion
  437.1 1.2 fusion.19
  (1 shorter events, 0.0 us)
Async XLA Ops:
  6.5 58.6 %all-gather.2.cloned.1.call-start = ((), (), s32[]{:S(2)}) async-start(), calls=%async_computation | async-start | bytes 1671168 | tf_op jit(solution)/shard_map/all_gather | solution.py:26
  7.3 235.6 %all-reduce.3.cloned.1.call-start = ((), (), s32[]{:S(2)}) async-start(), calls=%async_computation.1 | async-start | bytes 2097152
Sparse Core Ops, SparseCore 0:
  10.1 55.0 all-gather.1
  69.5 173.3 all-reduce.2
where the time goes:
time: 445 us
  waiting for transfers between devices  228 us (51%)
  blocking collectives  189 us (42%)
  between operations  14.1 us (3%)
  matrix products  8.89 us (2%)
    unnamed x3, waiting for transfers between devices  172 us
    psum x1, blocking collectives, body(): square_total = lax.psum(local_squares, 'dp')  139 us
    all_gather x1, waiting for transfers between devices, body(): lax.all_gather(latent, 'head', axis=1, tiled=True)  55.9 us
    all_gather x1, blocking collectives, body(): ortho = lax.all_gather(ortho_shard, 'dp', axis=0, tiled=True)  50 us
  transfers between devices with their start and end apart: 2, of which 2 were waited for; matrix products, arithmetic and copies ran while one was open for 1% of the time, Pallas kernels for 0%

commit v1 on v0

v1 whole, which is shorter than its diff:
```python
import jax
import jax.numpy as jnp
from jax import lax
from jax.experimental import pallas as pl
from jax.experimental.pallas import tpu as pltpu
from jax.sharding import Mesh, PartitionSpec as P

KV_RANK = 512
V_DIM = 128
ITERS = 5

epsilon = 1e-07
coef_one = 3.4445
coef_two = -4.775
coef_three = 2.0315

PIECE = 16
NN = (((1,), (0,)), ((), ()))
NT = (((1,), (1,)), ((), ()))


def partial_kernel(lengths_ref, latent_ref, own_ref, other_ref, out_ref):
    own_length = lengths_ref[lax.axis_index(("z", "y"))]
    core = lax.axis_index("c")
    columns, capacity = latent_ref.shape
    slot = lax.broadcasted_iota(jnp.int32, (columns, capacity), 1)
    live = jnp.where(slot < own_length, latent_ref[...], jnp.zeros((), jnp.bfloat16))
    heads = own_ref.shape[1] // V_DIM
    for grad_ref, owner in ((own_ref, core), (other_ref, 1 - core)):
        sums = lax.dot_general(live, grad_ref[...], NN, preferred_element_type=jnp.float32)
        sums = sums.astype(jnp.bfloat16)
        for block in range(columns // PIECE):
            for head in range(heads):
                out_ref[block * heads + head, owner] = sums[
                    block * PIECE : (block + 1) * PIECE, head * V_DIM : (head + 1) * V_DIM
                ]


def total_kernel(parts_ref, out_ref):
    shares = parts_ref.shape[0]
    total = jnp.sum(parts_ref[...].astype(jnp.float32), axis=0).astype(jnp.bfloat16)
    out_ref[...] = jnp.broadcast_to(total[None], (shares,) + total.shape)


def ortho_kernel(sums_ref, out_ref):
    heads = out_ref.shape[0]
    blocks = sums_ref.shape[0] // heads
    cores = sums_ref.shape[1]
    scale = 0.2 * max(KV_RANK, V_DIM) ** 0.5
    halves = 2
    ortho = []
    for head in range(heads):
        rows = [
            sums_ref[(chip * halves + half) * heads + head, core]
            for chip in range(blocks // halves)
            for core in range(cores)
            for half in range(halves)
        ]
        wide = jnp.concatenate(rows, axis=0).astype(jnp.float32)
        norm = jnp.sqrt(jnp.sum(wide * wide))
        wide = wide * (1.0 / (norm + epsilon))
        ortho.append(jnp.transpose(wide).astype(jnp.bfloat16))
    for step in range(ITERS):
        gram = [
            lax.dot_general(x, x, NT, preferred_element_type=jnp.float32).astype(jnp.bfloat16)
            for x in ortho
        ]
        squared = [lax.dot_general(a, a, NN, preferred_element_type=jnp.float32) for a in gram]
        poly = [
            (coef_two * a.astype(jnp.float32) + coef_three * s).astype(jnp.bfloat16)
            for a, s in zip(gram, squared)
        ]
        product = [
            lax.dot_general(b, x, NN, preferred_element_type=jnp.float32)
            for b, x in zip(poly, ortho)
        ]
        ortho = [
            (coef_one * x.astype(jnp.float32) + p).astype(jnp.bfloat16)
            for x, p in zip(ortho, product)
        ]
    for head in range(heads):
        out_ref[head] = jnp.transpose(scale * ortho[head].astype(jnp.float32)).astype(jnp.bfloat16)


def body(latent, value_grad, lengths):
    capacity, lat_cols = latent.shape
    heads = value_grad.shape[1] // V_DIM
    chips, cores, shares = lax.axis_size("x"), lax.axis_size("c"), lax.axis_size(("z", "y"))
    vmem = pl.BlockSpec(memory_space=pltpu.VMEM)
    smem = pl.BlockSpec(memory_space=pltpu.SMEM)

    other_grad = lax.ppermute(value_grad, "c", [(0, 1), (1, 0)])
    spread = jnp.broadcast_to(latent.T[None], (chips, lat_cols, capacity))
    gathered = lax.all_to_all(spread, "x", 0, 0, tiled=True)
    gathered = gathered.reshape(chips * lat_cols, capacity)

    partial = pl.pallas_call(
        partial_kernel,
        out_shape=jax.ShapeDtypeStruct((shares, cores, PIECE, V_DIM), jnp.bfloat16),
        in_specs=[smem, vmem, vmem, vmem],
        out_specs=vmem,
        compiler_params=pltpu.CompilerParams(vmem_limit_bytes=32 * 2**20),
    )(lengths, gathered, value_grad, other_grad)

    parts = lax.all_to_all(
        partial.reshape(shares * cores, PIECE, V_DIM), ("z", "y", "c"), 0, 0, tiled=True
    ).reshape(shares, cores, PIECE, V_DIM)

    total = pl.pallas_call(
        total_kernel,
        out_shape=jax.ShapeDtypeStruct(parts.shape, jnp.bfloat16),
        in_specs=[vmem],
        out_specs=vmem,
        compiler_params=pltpu.CompilerParams(vmem_limit_bytes=32 * 2**20),
    )(parts)

    sums = lax.all_to_all(total, ("z", "y"), 0, 0, tiled=True)

    return pl.pallas_call(
        ortho_kernel,
        out_shape=jax.ShapeDtypeStruct((heads, KV_RANK, V_DIM), jnp.bfloat16),
        in_specs=[vmem],
        out_specs=vmem,
        compiler_params=pltpu.CompilerParams(vmem_limit_bytes=32 * 2**20),
    )(sums)


def solution(mesh):
    grid = Mesh(mesh.devices.reshape(8, 8, 8, 2), ("z", "y", "x", "c"))
    return jax.shard_map(
        body,
        mesh=grid,
        in_specs=(P(("z", "y"), ("x", "c")), P(("z", "y"), ("x", "c")), P()),
        out_specs=P(("x", "c"), None, None),
        check_vma=False,
    )
```

time: 445 us -> 108 us (0.24)
  waiting for transfers between devices: 228 us -> 0.01 us
  blocking collectives: 189 us -> 98.7 us
  between operations: 14.1 us -> 0.04 us
  matrix products: 8.89 us -> 0 us
  Pallas kernels: 0 us -> 5.63 us
    unnamed x3 -> x0, waiting for transfers between devices: 172 us -> none
    psum x1 -> x0, blocking collectives: 139 us -> none  [body(): square_total = lax.psum(local_squares, 'dp')]
    all_to_all x0 -> x3, blocking collectives: none -> 98.7 us  [the longest x1 44.1 us: body(): lax.all_to_all(partial.reshape(shares * cores, PIECE, V_DIM), ('z', 'y',...]
    all_gather x1 -> x0, waiting for transfers between devices: 55.9 us -> none  [body(): lax.all_gather(latent, 'head', axis=1, tiled=True)]
    all_gather x1 -> x0, blocking collectives: 50 us -> none  [body(): ortho = lax.all_gather(ortho_shard, 'dp', axis=0, tiled=True)]
    dot_general x11 -> x0, matrix products: 8.89 us -> none  [the longest x1 4.18 us: body(): lax.dot_general(lax.all_gather(latent, 'head', axis=1, tiled=True), rows_...]
    pallas_call x0 -> x3, Pallas kernels: none -> 5.63 us  [the longest x1 3.99 us: body(): pl.pallas_call(ortho_kernel, out_shape=jax.ShapeDtypeStruct((heads, KV_RA...]
  transfers between devices with their start and end apart: 2 -> 1, of which waited for: 2 -> 0; matrix products, arithmetic and copies ran while one was open for 1% -> 1% of each run, Pallas kernels for 0% -> 0%
where the time goes in v1:
time: 108 us; the launch traced here: 107 us
  blocking collectives  98.7 us (91%)
  Pallas kernels  5.63 us (5%)
  starting transfers between devices  2.04 us (2%)
    all_to_all x1, blocking collectives, body(): lax.all_to_all(partial.reshape(shares * cores, PIECE, V_DIM), ('z', 'y',...  44.1 us
    all_to_all x1, blocking collectives, body(): gathered = lax.all_to_all(spread, 'x', 0, 0, tiled=True)  30.3 us
    all_to_all x1, blocking collectives, body(): sums = lax.all_to_all(total, ('z', 'y'), 0, 0, tiled=True)  24.3 us
    pallas_call x1, Pallas kernels, body(): pl.pallas_call(ortho_kernel, out_shape=jax.ShapeDtypeStruct((heads, KV_RA...  3.99 us
  transfers between devices with their start and end apart: 1, of which 0 were waited for; matrix products, arithmetic and copies ran while one was open for 1% of the time, Pallas kernels for 0%

profile of v1, /device:TPU:16, one launch (start us, length us, event | category | flops | bytes accessed | tf_op | source)
XLA Modules:
  0.0 107.4 jit_solution(14150493172857930361)
XLA Ops:
  0.0 0.0 copy-start
  0.0 0.0 copy-start.1
  0.0 2.0 %collective-permute-start = (bf16[1536,512]{1,0:T(8,128)(2,1)}, bf16[1536,512]{1,0:T(8,128)(2,1)S(1)}, u32[]{:S(2)}, u32[]{:S(2)}) collective-permute-start(bf16[1536,512]{1,0:T(8,128)(2,1)} %own_ref.1), channel_id=1, source_target_pairs={{0,1},{1,0},{2,3},{3,2},{4,5},{5,4},{6,7},{7,6},{8,9},{9,8},{10,11... | collective-permute-start | bytes 4718600 | tf_op jit(solution)/shard_map/ppermute | solution.py:92
  2.1 1.0 broadcast_in_dim.2
  3.0 30.3 %all_to_all.15 = bf16[8,32,1536]{2,1,0:T(8,128)(2,1)S(1)} all-to-all(bf16[8,32,1536]{2,1,0:T(8,128)(2,1)S(1)} %broadcast_in_dim.2), channel_id=1, replica_groups=mesh['z'=8,'y'=8,'x'=8,'c'=2] {'x'}, dimensions={0} | all-to-all | bytes 1572864 | tf_op jit(solution)/shard_map/all_to_all | solution.py:94
  33.3 0.0 collective-permute-done.other_ref
  33.3 0.0 copy-done
  33.3 0.0 copy-done.1
  33.4 1.5 %shard_map.37 = bf16[64,2,16,128]{3,2,1,0:T(8,128)(2,1)S(1)} custom-call(s32[64]{0:T(128)S(1)} %copy-done.1, bf16[256,1536]{1,0:T(8,128)(2,1)S(1)} %bitcast.4, bf16[1536,512]{1,0:T(8,128)(2,1)S(1)} %copy-done, bf16[1536,512]{1,0:T(8,128)(2,1)S(1)} %collective-permute-done.other_ref), custom_call_target="tpu_custom_call" | custom-call | tf_op jit(solution)/shard_map/pallas_call | solution.py:97
  34.9 44.1 %all_to_all.16 = bf16[128,16,128]{2,1,0:T(8,128)(2,1)S(1)} all-to-all(bf16[128,16,128]{2,1,0:T(8,128)(2,1)S(1)} %bitcast.5), channel_id=1, replica_groups=mesh['z'=8,'y'=8,'x'=8,'c'=2] {'z','y','c'}, dimensions={0} | all-to-all | bytes 1048576 | tf_op jit(solution)/shard_map/all_to_all | solution.py:105
  79.0 0.1 shard_map.38
  79.1 24.3 %all_to_all.17.sums_ref = bf16[64,2,16,128]{3,2,1,0:T(8,128)(2,1)S(1)} all-to-all(bf16[64,2,16,128]{3,2,1,0:T(8,128)(2,1)S(1)} %shard_map.38), channel_id=1, replica_groups=mesh['z'=8,'y'=8,'x'=8,'c'=2] {'z','y'}, dimensions={0} | all-to-all | bytes 1048576 | tf_op jit(solution)/shard_map/all_to_all | solution.py:117
  103.4 4.0 %shard_map.39 = bf16[4,512,128]{2,1,0:T(8,128)(2,1)} custom-call(bf16[64,2,16,128]{3,2,1,0:T(8,128)(2,1)S(1)} %all_to_all.17.sums_ref), custom_call_target="tpu_custom_call" | custom-call | tf_op jit(solution)/shard_map/pallas_call | solution.py:119
Async XLA Ops:
  0.0 33.3 %copy-start = (bf16[1536,512]{1,0:T(8,128)(2,1)S(1)}, bf16[1536,512]{1,0:T(8,128)(2,1)}, u32[]{:S(2)}) copy-start(bf16[1536,512]{1,0:T(8,128)(2,1)} %own_ref.1) | copy-start | bytes 4718596
  0.0 33.3 %copy-start.1 = (s32[64]{0:T(128)S(1)}, s32[64]{0:T(128)}, u32[]{:S(2)}) copy-start(s32[64]{0:T(128)} %lengths_ref.1) | copy-start | bytes 772
  0.0 33.3 %collective-permute-start = (bf16[1536,512]{1,0:T(8,128)(2,1)}, bf16[1536,512]{1,0:T(8,128)(2,1)S(1)}, u32[]{:S(2)}, u32[]{:S(2)}) collective-permute-start(bf16[1536,512]{1,0:T(8,128)(2,1)} %own_ref.1), channel_id=1, source_target_pairs={{0,1},{1,0},{2,3},{3,2},{4,5},{5,4},{6,7},{7,6},{8,9},{9,8},{10,11... | collective-permute-start | bytes 4718600 | tf_op jit(solution)/shard_map/ppermute | solution.py:92

commit v2 on v1

v2 whole, which is shorter than its diff:
```python
import jax
import jax.numpy as jnp
import numpy as np
from jax import lax
from jax.experimental import pallas as pl
from jax.experimental.pallas import tpu as pltpu
from jax.sharding import Mesh, PartitionSpec as P

KV_RANK = 512
V_DIM = 128
ITERS = 5

epsilon = 1e-07
coef_one = 3.4445
coef_two = -4.775
coef_three = 2.0315

SIDES = (8, 8, 8, 2)
AXES = ("z", "y", "x", "c")
NN = (((1,), (0,)), ((), ()))
NT = (((1,), (1,)), ((), ()))

VMEM = pl.BlockSpec(memory_space=pltpu.VMEM)
SMEM = pl.BlockSpec(memory_space=pltpu.SMEM)


def ring_groups(first_axis):
    index = np.arange(np.prod(SIDES)).reshape(SIDES)
    rings = []
    for core in range(2):
        axis = first_axis if core == 0 else 1 - first_axis
        rings += np.moveaxis(index[..., core], axis, -1).reshape(-1, SIDES[axis]).tolist()
    return rings


def exchange(blocks, groups):
    return lax.all_to_all(blocks, AXES, 0, 0, axis_index_groups=groups, tiled=True)


def run_kernel(kernel, shape, specs, *operands, flops=0):
    size = 2 * int(np.prod(shape))
    return pl.pallas_call(
        kernel,
        out_shape=jax.ShapeDtypeStruct(shape, jnp.bfloat16),
        in_specs=specs,
        out_specs=VMEM,
        cost_estimate=pl.CostEstimate(flops=flops, bytes_accessed=2 * size, transcendentals=0),
        compiler_params=pltpu.CompilerParams(vmem_limit_bytes=32 * 2**20),
    )(*operands)


def masked_product(lengths_ref, latent_ref, grad_ref):
    own_length = lengths_ref[lax.axis_index(("z", "y"))]
    slot = lax.broadcasted_iota(jnp.int32, latent_ref.shape, 1)
    live = jnp.where(slot < own_length, latent_ref[...], jnp.zeros((), jnp.bfloat16))
    sums = lax.dot_general(live, grad_ref[...], NN, preferred_element_type=jnp.float32)
    return sums.astype(jnp.bfloat16)


def own_kernel(lengths_ref, latent_ref, grad_ref, out_ref):
    sums = masked_product(lengths_ref, latent_ref, grad_ref)
    for head in range(out_ref.shape[0]):
        out_ref[head] = sums[:, head * V_DIM : (head + 1) * V_DIM]


def other_kernel(lengths_ref, latent_ref, grad_ref, own_ref, out_ref):
    heads = own_ref.shape[0]
    out_ref[:heads] = own_ref[...]
    sums = masked_product(lengths_ref, latent_ref, grad_ref)
    for head in range(heads):
        out_ref[heads + head] = sums[:, head * V_DIM : (head + 1) * V_DIM]


def total_kernel(parts_ref, out_ref):
    total = jnp.sum(parts_ref[...].astype(jnp.float32), axis=0).astype(jnp.bfloat16)
    out_ref[...] = jnp.broadcast_to(total[None], out_ref.shape)


def ortho_kernel(sums_ref, out_ref):
    heads, chips, cores, columns, _ = out_ref.shape
    core = lax.axis_index("c")
    scale = 0.2 * max(KV_RANK, V_DIM) ** 0.5
    ortho = []
    for head in range(heads):
        rows = [sums_ref[part * heads + head] for part in range(cores)]
        wide = jnp.concatenate(rows, axis=0).astype(jnp.float32)
        norm = jnp.sqrt(jnp.sum(wide * wide))
        wide = wide * (1.0 / (norm + epsilon))
        ortho.append(jnp.transpose(wide).astype(jnp.bfloat16))
    for step in range(ITERS):
        gram = [
            lax.dot_general(x, x, NT, preferred_element_type=jnp.float32).astype(jnp.bfloat16)
            for x in ortho
        ]
        squared = [lax.dot_general(a, a, NN, preferred_element_type=jnp.float32) for a in gram]
        poly = [
            (coef_two * a.astype(jnp.float32) + coef_three * s).astype(jnp.bfloat16)
            for a, s in zip(gram, squared)
        ]
        product = [
            lax.dot_general(b, x, NN, preferred_element_type=jnp.float32)
            for b, x in zip(poly, ortho)
        ]
        ortho = [
            (coef_one * x.astype(jnp.float32) + p).astype(jnp.bfloat16)
            for x, p in zip(ortho, product)
        ]
    for head in range(heads):
        wide = jnp.transpose(scale * ortho[head].astype(jnp.float32)).astype(jnp.bfloat16)
        for part in range(cores):
            owner = core if part == 0 else 1 - core
            for chip in range(chips):
                start = (part * chips + chip) * columns
                out_ref[head, chip, owner] = wide[start : start + columns]


def body(latent, value_grad, lengths):
    capacity, columns = latent.shape
    heads = value_grad.shape[1] // V_DIM
    chips, cores = lax.axis_size("x"), lax.axis_size("c")
    rows = chips * columns
    flops = 2 * rows * capacity * heads * V_DIM
    first, second = ring_groups(1), ring_groups(0)

    gathered = lax.all_gather(latent.T, "x", axis=0, tiled=True)
    swapped = lax.ppermute(gathered, "c", [(0, 1), (1, 0)])
    specs = [SMEM, VMEM, VMEM]
    own = run_kernel(
        own_kernel, (heads, rows, V_DIM), specs, lengths, gathered, value_grad, flops=flops
    )
    blocks = run_kernel(
        other_kernel,
        (cores * heads, rows, V_DIM),
        specs + [VMEM],
        lengths,
        swapped,
        value_grad,
        own,
        flops=flops,
    )
    parts = exchange(blocks, first)
    parts = exchange(run_kernel(total_kernel, parts.shape, [VMEM], parts), second)
    sums = exchange(run_kernel(total_kernel, parts.shape, [VMEM], parts), first)
    update = run_kernel(ortho_kernel, (heads, chips, cores, columns, V_DIM), [VMEM], sums)
    return update.reshape(heads, KV_RANK, V_DIM)


def solution(mesh):
    return jax.shard_map(
        body,
        mesh=Mesh(mesh.devices.reshape(SIDES), AXES),
        in_specs=(P(("z", "y"), ("x", "c")), P(("z", "y"), ("x", "c")), P()),
        out_specs=P(("x", "c"), None, None),
        check_vma=False,
    )
```

time: 108 us -> 104 us (0.963)
  the two profiles are of different devices: /device:TPU:16 before, /device:TPU:4 now
where the time goes in v2:
time: 104 us
  blocking collectives  93.4 us (90%)
  Pallas kernels  6.36 us (6%)
  local copies, waits for them, and re-layouts  2.34 us (2%)
  starting transfers between devices  1.91 us (2%)
    all_to_all x3, blocking collectives, exchange(): lax.all_to_all(blocks, AXES, 0, 0, axis_index_groups=groups, tiled=True)  56.8 us
    all_gather x1, blocking collectives, body(): gathered = lax.all_gather(latent.T, 'x', axis=0, tiled=True)  36.6 us
    pallas_call x5, Pallas kernels, run_kernel(): pl.pallas_call(kernel, out_shape=jax.ShapeDtypeStruct(shape, jnp.bfloat16...  6.36 us
    unnamed x6, local copies, waits for them, and re-layouts  2.34 us
  transfers between devices with their start and end apart: 1, of which 0 were waited for; matrix products, arithmetic and copies ran while one was open for 0% of the time, Pallas kernels for 1%

profile of v2, /device:TPU:4, one launch (start us, length us, event | category | flops | bytes accessed | tf_op | source)
XLA Modules:
  0.0 104.1 jit_solution(10138303371855046152)
XLA Ops:
  0.0 36.6 %all_gather.3.latent_ref = bf16[256,1536]{1,0:T(8,128)(2,1)S(1)} all-gather(bf16[32,1536]{1,0:T(8,128)(2,1)} %bitcast.2), channel_id=1, replica_groups=mesh['z'=8,'y'=8,'x'=8,'c'=2] {'x'}, dimensions={0}, use_global_device_ids=true | all-gather | bytes 884736 | tf_op jit(solution)/shard_map/all_gather | solution.py:125
  36.6 1.9 %collective-permute-start = (bf16[256,1536]{1,0:T(8,128)(2,1)S(1)}, bf16[256,1536]{1,0:T(8,128)(2,1)S(1)}, u32[]{:S(2)}, u32[]{:S(2)}) collective-permute-start(bf16[256,1536]{1,0:T(8,128)(2,1)S(1)} %all_gather.3.latent_ref), channel_id=1, source_target_pairs={{0,1},{1,0},{2,3},{3,2},{4,5},{5,4},{6,7},{7,6},{8,9},{9,8},{10,11... | collective-permute-start | bytes 2359304 | tf_op jit(solution)/shard_map/ppermute | solution.py:126
  38.5 0.0 copy-start
  38.5 1.4 %copy-done = bf16[1536,512]{1,0:T(8,128)(2,1)S(1)} copy-done((bf16[1536,512]{1,0:T(8,128)(2,1)S(1)}, bf16[1536,512]{1,0:T(8,128)(2,1)}, u32[]{:S(2)}) %copy-start) | copy-done | bytes 1572888
  39.9 0.0 copy-start.2
  39.9 0.7 copy-done.2
  40.5 0.0 copy-start.1
  40.5 1.1 %shard_map.37.own_ref = bf16[4,256,128]{2,1,0:T(8,128)(2,1)S(1)} custom-call(s32[64]{0:T(128)S(1)} %copy-done.2, bf16[256,1536]{1,0:T(8,128)(2,1)S(1)} %all_gather.3.latent_ref, bf16[1536,512]{1,0:T(8,128)(2,1)S(1)} %copy-done), custom_call_target="tpu_custom_call" | custom-call | flops 402653184 | bytes 524288 | tf_op jit(solution)/shard_map/pallas_call | solution.py:42
  41.7 0.0 collective-permute-done.latent_ref
  41.7 0.3 copy-done.1
  42.0 1.1 %shard_map.38 = bf16[8,256,128]{2,1,0:T(8,128)(2,1)S(1)} custom-call(s32[64]{0:T(128)S(1)} %copy-done.2, bf16[256,1536]{1,0:T(8,128)(2,1)S(1)} %collective-permute-done.latent_ref, bf16[1536,512]{1,0:T(8,128)(2,1)S(1)} %copy-done.1, bf16[4,256,128]{2,1,0:T(8,128)(2,1)S(1)} %shard_map.37.own_ref), custom_call_target="tpu_custom_call" | custom-call | flops 402653184 | bytes 1048576 | tf_op jit(solution)/shard_map/pallas_call | solution.py:42
  43.1 15.7 %all_to_all.15.parts_ref = bf16[8,256,128]{2,1,0:T(8,128)(2,1)S(1)} all-to-all(bf16[8,256,128]{2,1,0:T(8,128)(2,1)S(1)} %shard_map.38), channel_id=1, replica_groups={{0,16,32,48,64,80,96,112},{2,18,34,50,66,82,98,114},{4,20,36,52,68,84,1..., dimensions={0} | all-to-all | bytes 1048576 | tf_op jit(solution)/shard_map/all_to_all | solution.py:37
  58.8 0.1 shard_map.39
  58.9 25.5 %all_to_all.16.parts_ref = bf16[8,256,128]{2,1,0:T(8,128)(2,1)S(1)} all-to-all(bf16[8,256,128]{2,1,0:T(8,128)(2,1)S(1)} %shard_map.39), channel_id=1, replica_groups={{0,128,256,384,512,640,768,896},{2,130,258,386,514,642,770,898},{4,132,..., dimensions={0} | all-to-all | bytes 1048576 | tf_op jit(solution)/shard_map/all_to_all | solution.py:37
  84.3 0.1 shard_map.40
  84.4 15.7 %all_to_all.17.sums_ref = bf16[8,256,128]{2,1,0:T(8,128)(2,1)S(1)} all-to-all(bf16[8,256,128]{2,1,0:T(8,128)(2,1)S(1)} %shard_map.40), channel_id=1, replica_groups={{0,16,32,48,64,80,96,112},{2,18,34,50,66,82,98,114},{4,20,36,52,68,84,1..., dimensions={0} | all-to-all | bytes 1048576 | tf_op jit(solution)/shard_map/all_to_all | solution.py:37
  100.1 4.0 %shard_map.41 = bf16[4,8,2,32,128]{4,3,2,1,0:T(8,128)(2,1)} custom-call(bf16[8,256,128]{2,1,0:T(8,128)(2,1)S(1)} %all_to_all.17.sums_ref), custom_call_target="tpu_custom_call" | custom-call | bytes 1048576 | tf_op jit(solution)/shard_map/pallas_call | solution.py:42
Async XLA Ops:
  36.6 5.1 %collective-permute-start = (bf16[256,1536]{1,0:T(8,128)(2,1)S(1)}, bf16[256,1536]{1,0:T(8,128)(2,1)S(1)}, u32[]{:S(2)}, u32[]{:S(2)}) collective-permute-start(bf16[256,1536]{1,0:T(8,128)(2,1)S(1)} %all_gather.3.latent_ref), channel_id=1, source_target_pairs={{0,1},{1,0},{2,3},{3,2},{4,5},{5,4},{6,7},{7,6},{8,9},{9,8},{10,11... | collective-permute-start | bytes 2359304 | tf_op jit(solution)/shard_map/ppermute | solution.py:126
  38.5 1.4 %copy-start = (bf16[1536,512]{1,0:T(8,128)(2,1)S(1)}, bf16[1536,512]{1,0:T(8,128)(2,1)}, u32[]{:S(2)}) copy-start(bf16[1536,512]{1,0:T(8,128)(2,1)} %grad_ref.3) | copy-start | bytes 4718596
  39.9 0.7 copy-start.2
  40.5 1.4 %copy-start.1 = (bf16[1536,512]{1,0:T(8,128)(2,1)S(1)}, bf16[1536,512]{1,0:T(8,128)(2,1)}, u32[]{:S(2)}) copy-start(bf16[1536,512]{1,0:T(8,128)(2,1)} %grad_ref.3) | copy-start | bytes 4718596

commit v3 on v2

v3 whole, which is shorter than its diff:
```python
import jax
import jax.numpy as jnp
import numpy as np
from jax import lax
from jax.experimental import pallas as pl
from jax.experimental.pallas import tpu as pltpu
from jax.sharding import Mesh, PartitionSpec as P

KV_RANK = 512
V_DIM = 128
ITERS = 5

epsilon = 1e-07
coef_one = 3.4445
coef_two = -4.775
coef_three = 2.0315

LANES = 128
LATENT_MAX = 16.0
HEADROOM = 10.0

SIDES = (8, 8, 8, 2)
AXES = ("z", "y", "x", "c")
NN = (((1,), (0,)), ((), ()))
NT = (((1,), (1,)), ((), ()))

VMEM = pl.BlockSpec(memory_space=pltpu.VMEM)
SMEM = pl.BlockSpec(memory_space=pltpu.SMEM)


def ring_groups(first_axis):
    index = np.arange(np.prod(SIDES)).reshape(SIDES)
    rings = []
    for core in range(2):
        axis = first_axis if core == 0 else 1 - first_axis
        rings += np.moveaxis(index[..., core], axis, -1).reshape(-1, SIDES[axis]).tolist()
    return rings


def exchange(blocks, groups):
    return lax.all_to_all(blocks, AXES, 0, 0, axis_index_groups=groups, tiled=True)


def run_kernel(kernel, shape, specs, *operands):
    return pl.pallas_call(
        kernel,
        out_shape=jax.ShapeDtypeStruct(shape, jnp.bfloat16),
        in_specs=specs,
        out_specs=VMEM,
        compiler_params=pltpu.CompilerParams(vmem_limit_bytes=32 * 2**20),
    )(*operands)


def encode_kernel(lengths_ref, latent_ref, out_ref):
    columns, capacity = latent_ref.shape
    own_length = lengths_ref[lax.axis_index(("z", "y"))]
    slot = lax.broadcasted_iota(jnp.int32, (columns, capacity), 1)
    live = jnp.where(slot < own_length, latent_ref[...].astype(jnp.float32), 0.0)
    largest = jnp.max(jnp.abs(live), axis=1, keepdims=True)
    shift = jnp.floor(jnp.log(LATENT_MAX / largest) * (1.0 / np.log(2.0)))
    shift = jnp.clip(shift, 0.0, 110.0)
    scaled = live * jnp.exp2(shift + HEADROOM)
    out_ref[:, :capacity] = scaled.astype(jnp.bfloat16)
    out_ref[:, capacity:] = jnp.broadcast_to(shift, (columns, LANES)).astype(jnp.bfloat16)


def partial_kernel(latent_ref, grad_ref, out_ref):
    capacity = grad_ref.shape[0]
    blocks, rows, _ = out_ref.shape
    heads = grad_ref.shape[1] // V_DIM
    for part in range(blocks // heads):
        here = slice(part * rows, (part + 1) * rows)
        sums = lax.dot_general(
            latent_ref[here, :capacity], grad_ref[...], NN, preferred_element_type=jnp.float32
        )
        shift = latent_ref[here, capacity:].astype(jnp.float32)[:, :1]
        sums = (sums * jnp.exp2(-HEADROOM - shift)).astype(jnp.bfloat16)
        for head in range(heads):
            out_ref[part * heads + head] = sums[:, head * V_DIM : (head + 1) * V_DIM]


def total_kernel(parts_ref, out_ref):
    total = jnp.sum(parts_ref[...].astype(jnp.float32), axis=0).astype(jnp.bfloat16)
    out_ref[...] = jnp.broadcast_to(total[None], out_ref.shape)


def ortho_kernel(sums_ref, out_ref):
    heads = out_ref.shape[0]
    parts = sums_ref.shape[0] // heads
    scale = 0.2 * max(KV_RANK, V_DIM) ** 0.5
    ortho = []
    for head in range(heads):
        rows = [sums_ref[part * heads + head] for part in range(parts)]
        wide = jnp.concatenate(rows, axis=0).astype(jnp.float32)
        norm = jnp.sqrt(jnp.sum(wide * wide))
        wide = wide * (1.0 / (norm + epsilon))
        ortho.append(jnp.transpose(wide).astype(jnp.bfloat16))
    for step in range(ITERS):
        gram = [
            lax.dot_general(x, x, NT, preferred_element_type=jnp.float32).astype(jnp.bfloat16)
            for x in ortho
        ]
        squared = [lax.dot_general(a, a, NN, preferred_element_type=jnp.float32) for a in gram]
        poly = [
            (coef_two * a.astype(jnp.float32) + coef_three * s).astype(jnp.bfloat16)
            for a, s in zip(gram, squared)
        ]
        product = [
            lax.dot_general(b, x, NN, preferred_element_type=jnp.float32)
            for b, x in zip(poly, ortho)
        ]
        ortho = [
            (coef_one * x.astype(jnp.float32) + p).astype(jnp.bfloat16)
            for x, p in zip(ortho, product)
        ]
    for head in range(heads):
        out_ref[head] = jnp.transpose(scale * ortho[head].astype(jnp.float32)).astype(jnp.bfloat16)


def body(latent, value_grad, lengths):
    capacity, columns = latent.shape
    heads = value_grad.shape[1] // V_DIM
    first, second = ring_groups(1), ring_groups(0)

    coded = run_kernel(encode_kernel, (columns, capacity + LANES), [SMEM, VMEM], lengths, latent.T)
    gathered = lax.all_gather(coded.astype(jnp.float16), ("x", "c"), axis=0, tiled=True)
    blocks = run_kernel(
        partial_kernel,
        (2 * heads, KV_RANK // 2, V_DIM),
        [VMEM, VMEM],
        gathered.astype(jnp.bfloat16),
        value_grad,
    )
    parts = exchange(blocks, first)
    parts = exchange(run_kernel(total_kernel, parts.shape, [VMEM], parts), second)
    sums = exchange(run_kernel(total_kernel, parts.shape, [VMEM], parts), first)
    return run_kernel(ortho_kernel, (heads, KV_RANK, V_DIM), [VMEM], sums)


def solution(mesh):
    return jax.shard_map(
        body,
        mesh=Mesh(mesh.devices.reshape(SIDES), AXES),
        in_specs=(P(("z", "y"), ("x", "c")), P(("z", "y"), ("x", "c")), P()),
        out_specs=P(("x", "c"), None, None),
        check_vma=False,
    )
```

time: 104 us -> 96 us (0.923)
  the two profiles are of different devices: /device:TPU:4 before, /device:TPU:2 now
where the time goes in v3:
time: 96 us; the launch traced here: 95.7 us
  blocking collectives  86.9 us (91%)
  Pallas kernels  5.77 us (6%)
  local copies, waits for them, and re-layouts  2.73 us (3%)
    all_to_all x3, blocking collectives, exchange(): lax.all_to_all(blocks, AXES, 0, 0, axis_index_groups=groups, tiled=True)  54.9 us
    all_gather x1, blocking collectives, body(): lax.all_gather(coded.astype(jnp.float16), ('x', 'c'), axis=0, tiled=True)  32 us
    pallas_call x5, Pallas kernels, run_kernel(): pl.pallas_call(kernel, out_shape=jax.ShapeDtypeStruct(shape, jnp.bfloat16...  5.77 us
    unnamed x6, local copies, waits for them, and re-layouts  2.73 us

profile of v3, /device:TPU:2, one launch (start us, length us, event | category | flops | bytes accessed | tf_op | source)
XLA Modules:
  0.0 95.7 jit_solution(10284679730786648251)
XLA Ops:
  0.0 0.0 copy-start.1
  0.0 0.9 copy-done.1
  0.9 0.0 copy-start.2
  0.9 0.7 copy-done.2
  1.5 0.7 shard_map.37
  2.3 32.0 %all-gather.1 = f16[512,1664]{1,0:T(8,128)(2,1)S(1)} all-gather(f16[32,1664]{1,0:T(8,128)(2,1)S(1)} %convert_element_type.6), channel_id=1, replica_groups=mesh['z'=8,'y'=8,'x'=8,'c'=2] {'x','c'}, dimensions={0}, use_global_device_ids=true | all-gather | bytes 1810432 | tf_op jit(solution)/shard_map/all_gather | solution.py:126
  34.3 0.0 copy-start
  34.3 0.2 convert_element_type.7.latent_ref
  34.5 1.2 %copy-done = bf16[1536,512]{1,0:T(8,128)(2,1)S(1)} copy-done((bf16[1536,512]{1,0:T(8,128)(2,1)S(1)}, bf16[1536,512]{1,0:T(8,128)(2,1)}, u32[]{:S(2)}) %copy-start) | copy-done | bytes 1572888
  35.7 1.0 %shard_map.38 = bf16[8,256,128]{2,1,0:T(8,128)(2,1)S(1)} custom-call(bf16[512,1664]{1,0:T(8,128)(2,1)S(1)} %convert_element_type.7.latent_ref, bf16[1536,512]{1,0:T(8,128)(2,1)S(1)} %copy-done), custom_call_target="tpu_custom_call" | custom-call | tf_op jit(solution)/shard_map/pallas_call | solution.py:45
  36.6 15.7 %all_to_all.15.parts_ref = bf16[8,256,128]{2,1,0:T(8,128)(2,1)S(1)} all-to-all(bf16[8,256,128]{2,1,0:T(8,128)(2,1)S(1)} %shard_map.38), channel_id=1, replica_groups={{0,16,32,48,64,80,96,112},{2,18,34,50,66,82,98,114},{4,20,36,52,68,84,1..., dimensions={0} | all-to-all | bytes 1048576 | tf_op jit(solution)/shard_map/all_to_all | solution.py:41
  52.3 0.1 shard_map.39
  52.4 23.5 %all_to_all.16.parts_ref = bf16[8,256,128]{2,1,0:T(8,128)(2,1)S(1)} all-to-all(bf16[8,256,128]{2,1,0:T(8,128)(2,1)S(1)} %shard_map.39), channel_id=1, replica_groups={{0,128,256,384,512,640,768,896},{2,130,258,386,514,642,770,898},{4,132,..., dimensions={0} | all-to-all | bytes 1048576 | tf_op jit(solution)/shard_map/all_to_all | solution.py:41
  76.0 0.1 shard_map.40
  76.0 15.7 %all_to_all.17.sums_ref = bf16[8,256,128]{2,1,0:T(8,128)(2,1)S(1)} all-to-all(bf16[8,256,128]{2,1,0:T(8,128)(2,1)S(1)} %shard_map.40), channel_id=1, replica_groups={{0,16,32,48,64,80,96,112},{2,18,34,50,66,82,98,114},{4,20,36,52,68,84,1..., dimensions={0} | all-to-all | bytes 1048576 | tf_op jit(solution)/shard_map/all_to_all | solution.py:41
  91.7 4.0 %shard_map.41 = bf16[4,512,128]{2,1,0:T(8,128)(2,1)} custom-call(bf16[8,256,128]{2,1,0:T(8,128)(2,1)S(1)} %all_to_all.17.sums_ref), custom_call_target="tpu_custom_call" | custom-call | tf_op jit(solution)/shard_map/pallas_call | solution.py:45
  (1 shorter events, 0.0 us)
Async XLA Ops:
  0.0 0.9 copy-start.1
  0.9 0.7 copy-start.2
  34.3 1.4 %copy-start = (bf16[1536,512]{1,0:T(8,128)(2,1)S(1)}, bf16[1536,512]{1,0:T(8,128)(2,1)}, u32[]{:S(2)}) copy-start(bf16[1536,512]{1,0:T(8,128)(2,1)} %grad_ref.1) | copy-start | bytes 4718596

commit v4 on v3

--- a/solution.py
+++ b/solution.py
@@ -28,13 +28,23 @@
 SMEM = pl.BlockSpec(memory_space=pltpu.SMEM)
 
 
-def ring_groups(first_axis):
+ORDER = [0, 4, 3, 7, 1, 5, 2, 6]
+PAIR = 1
+
+
+def stage_groups():
     index = np.arange(np.prod(SIDES)).reshape(SIDES)
-    rings = []
+    wide, narrow = [], []
     for core in range(2):
-        axis = first_axis if core == 0 else 1 - first_axis
-        rings += np.moveaxis(index[..., core], axis, -1).reshape(-1, SIDES[axis]).tolist()
-    return rings
+        plane = index[..., core] if core == 0 else index[..., core].swapaxes(0, 1)
+        for column in range(SIDES[2]):
+            for start in range(0, SIDES[0], PAIR):
+                ring = plane[start : start + PAIR, ORDER, column]
+                wide.append(ring.reshape(-1).tolist())
+            for place in range(SIDES[1]):
+                for start in range(PAIR):
+                    narrow.append(plane[start::PAIR, place, column][ORDER].tolist())
+    return wide, narrow
 
 
 def exchange(blocks, groups):
@@ -70,9 +80,8 @@
     heads = grad_ref.shape[1] // V_DIM
     for part in range(blocks // heads):
         here = slice(part * rows, (part + 1) * rows)
-        sums = lax.dot_general(
-            latent_ref[here, :capacity], grad_ref[...], NN, preferred_element_type=jnp.float32
-        )
+        coded = latent_ref[here, :capacity]
+        sums = lax.dot_general(coded, grad_ref[...], NN, preferred_element_type=jnp.float32)
         shift = latent_ref[here, capacity:].astype(jnp.float32)[:, :1]
         sums = (sums * jnp.exp2(-HEADROOM - shift)).astype(jnp.bfloat16)
         for head in range(heads):
@@ -88,18 +97,22 @@
     heads = out_ref.shape[0]
     parts = sums_ref.shape[0] // heads
     scale = 0.2 * max(KV_RANK, V_DIM) ** 0.5
-    ortho = []
-    for head in range(heads):
-        rows = [sums_ref[part * heads + head] for part in range(parts)]
-        wide = jnp.concatenate(rows, axis=0).astype(jnp.float32)
-        norm = jnp.sqrt(jnp.sum(wide * wide))
-        wide = wide * (1.0 / (norm + epsilon))
-        ortho.append(jnp.transpose(wide).astype(jnp.bfloat16))
+    sums = [
+        jnp.concatenate([sums_ref[part * heads + head] for part in range(parts)], axis=0)
+        for head in range(heads)
+    ]
+    turned = [jnp.transpose(g) for g in sums]
+    gram = [lax.dot_general(t, t, NT, preferred_element_type=jnp.float32) for t in turned]
+    wide = [g.astype(jnp.float32) for g in sums]
+    inverse = [1.0 / (jnp.sqrt(jnp.sum(w * w)) + epsilon) for w in wide]
+    gram = [(a * (i * i)).astype(jnp.bfloat16) for a, i in zip(gram, inverse)]
+    ortho = [(t.astype(jnp.float32) * i).astype(jnp.bfloat16) for t, i in zip(turned, inverse)]
     for step in range(ITERS):
-        gram = [
-            lax.dot_general(x, x, NT, preferred_element_type=jnp.float32).astype(jnp.bfloat16)
-            for x in ortho
-        ]
+        if step:
+            gram = [
+                lax.dot_general(x, x, NT, preferred_element_type=jnp.float32).astype(jnp.bfloat16)
+                for x in ortho
+            ]
         squared = [lax.dot_general(a, a, NN, preferred_element_type=jnp.float32) for a in gram]
         poly = [
             (coef_two * a.astype(jnp.float32) + coef_three * s).astype(jnp.bfloat16)
@@ -120,20 +133,22 @@
 def body(latent, value_grad, lengths):
     capacity, columns = latent.shape
     heads = value_grad.shape[1] // V_DIM
-    first, second = ring_groups(1), ring_groups(0)
+    wide, narrow = stage_groups()
 
     coded = run_kernel(encode_kernel, (columns, capacity + LANES), [SMEM, VMEM], lengths, latent.T)
     gathered = lax.all_gather(coded.astype(jnp.float16), ("x", "c"), axis=0, tiled=True)
+    members, others = len(wide[0]), len(narrow[0])
+    block = (KV_RANK * heads // members, V_DIM)
     blocks = run_kernel(
         partial_kernel,
-        (2 * heads, KV_RANK // 2, V_DIM),
+        (members, *block),
         [VMEM, VMEM],
         gathered.astype(jnp.bfloat16),
         value_grad,
     )
-    parts = exchange(blocks, first)
-    parts = exchange(run_kernel(total_kernel, parts.shape, [VMEM], parts), second)
-    sums = exchange(run_kernel(total_kernel, parts.shape, [VMEM], parts), first)
+    parts = exchange(blocks, wide)
+    parts = exchange(run_kernel(total_kernel, (others, *block), [VMEM], parts), narrow)
+    sums = exchange(run_kernel(total_kernel, (members, *block), [VMEM], parts), wide)
     return run_kernel(ortho_kernel, (heads, KV_RANK, V_DIM), [VMEM], sums)
 
 

time: 96 us -> 90.8 us (0.946)
  the two profiles are of different devices: /device:TPU:2 before, /device:TPU:32 now
where the time goes in v4:
time: 90.8 us; the launch traced here: 90.5 us
  blocking collectives  82 us (90%)
  Pallas kernels  5.47 us (6%)
  local copies, waits for them, and re-layouts  2.73 us (3%)
    all_to_all x3, blocking collectives, exchange(): lax.all_to_all(blocks, AXES, 0, 0, axis_index_groups=groups, tiled=True)  60.3 us
    all_gather x1, blocking collectives, body(): lax.all_gather(coded.astype(jnp.float16), ('x', 'c'), axis=0, tiled=True)  21.7 us
    pallas_call x5, Pallas kernels, run_kernel(): pl.pallas_call(kernel, out_shape=jax.ShapeDtypeStruct(shape, jnp.bfloat16...  5.47 us
    unnamed x6, local copies, waits for them, and re-layouts  2.73 us

profile of v4, /device:TPU:32, one launch (start us, length us, event | category | flops | bytes accessed | tf_op | source)
XLA Modules:
  0.0 90.5 jit_solution(5610225886169932085)
XLA Ops:
  0.0 0.0 copy-start.1
  0.0 0.9 copy-done.1
  0.9 0.0 copy-start.2
  0.9 0.7 copy-done.2
  1.5 0.7 shard_map.37
  2.3 21.7 %all-gather.1 = f16[512,1664]{1,0:T(8,128)(2,1)S(1)} all-gather(f16[32,1664]{1,0:T(8,128)(2,1)S(1)} %convert_element_type.6), channel_id=1, replica_groups=mesh['z'=8,'y'=8,'x'=8,'c'=2] {'x','c'}, dimensions={0}, use_global_device_ids=true | all-gather | bytes 1810432 | tf_op jit(solution)/shard_map/all_gather | solution.py:139
  23.9 0.0 copy-start
  23.9 0.2 convert_element_type.7.latent_ref
  24.2 1.2 %copy-done = bf16[1536,512]{1,0:T(8,128)(2,1)S(1)} copy-done((bf16[1536,512]{1,0:T(8,128)(2,1)S(1)}, bf16[1536,512]{1,0:T(8,128)(2,1)}, u32[]{:S(2)}) %copy-start) | copy-done | bytes 1572888
  25.4 1.0 %shard_map.38 = bf16[8,256,128]{2,1,0:T(8,128)(2,1)S(1)} custom-call(bf16[512,1664]{1,0:T(8,128)(2,1)S(1)} %convert_element_type.7.latent_ref, bf16[1536,512]{1,0:T(8,128)(2,1)S(1)} %copy-done), custom_call_target="tpu_custom_call" | custom-call | tf_op jit(solution)/shard_map/pallas_call | solution.py:55
  26.3 24.7 %all_to_all.15.parts_ref = bf16[8,256,128]{2,1,0:T(8,128)(2,1)S(1)} all-to-all(bf16[8,256,128]{2,1,0:T(8,128)(2,1)S(1)} %shard_map.38), channel_id=1, replica_groups={{0,64,48,112,16,80,32,96},{128,192,176,240,144,208,160,224},{256,320,30..., dimensions={0} | all-to-all | bytes 1048576 | tf_op jit(solution)/shard_map/all_to_all | solution.py:51
  51.0 0.1 shard_map.39
  51.1 20.7 %all_to_all.16.parts_ref = bf16[8,256,128]{2,1,0:T(8,128)(2,1)S(1)} all-to-all(bf16[8,256,128]{2,1,0:T(8,128)(2,1)S(1)} %shard_map.39), channel_id=1, replica_groups={{0,512,384,896,128,640,256,768},{16,528,400,912,144,656,272,784},{32,54..., dimensions={0} | all-to-all | bytes 1048576 | tf_op jit(solution)/shard_map/all_to_all | solution.py:51
  71.8 0.1 shard_map.40
  71.8 15.0 %all_to_all.17.sums_ref = bf16[8,256,128]{2,1,0:T(8,128)(2,1)S(1)} all-to-all(bf16[8,256,128]{2,1,0:T(8,128)(2,1)S(1)} %shard_map.40), channel_id=1, replica_groups={{0,64,48,112,16,80,32,96},{128,192,176,240,144,208,160,224},{256,320,30..., dimensions={0} | all-to-all | bytes 1048576 | tf_op jit(solution)/shard_map/all_to_all | solution.py:51
  86.8 3.7 %shard_map.41 = bf16[4,512,128]{2,1,0:T(8,128)(2,1)} custom-call(bf16[8,256,128]{2,1,0:T(8,128)(2,1)S(1)} %all_to_all.17.sums_ref), custom_call_target="tpu_custom_call" | custom-call | tf_op jit(solution)/shard_map/pallas_call | solution.py:55
  (1 shorter events, 0.0 us)
Async XLA Ops:
  0.0 0.9 copy-start.1
  0.9 0.7 copy-start.2
  23.9 1.4 %copy-start = (bf16[1536,512]{1,0:T(8,128)(2,1)S(1)}, bf16[1536,512]{1,0:T(8,128)(2,1)}, u32[]{:S(2)}) copy-start(bf16[1536,512]{1,0:T(8,128)(2,1)} %grad_ref.1) | copy-start | bytes 4718596

commit v5 on v4

--- a/solution.py
+++ b/solution.py
@@ -93,7 +93,7 @@
     out_ref[...] = jnp.broadcast_to(total[None], out_ref.shape)
 
 
-def ortho_kernel(sums_ref, out_ref):
+def ortho_kernel(sums_ref, out_hbm, out_ref, sent):
     heads = out_ref.shape[0]
     parts = sums_ref.shape[0] // heads
     scale = 0.2 * max(KV_RANK, V_DIM) ** 0.5
@@ -126,8 +126,13 @@
             (coef_one * x.astype(jnp.float32) + p).astype(jnp.bfloat16)
             for x, p in zip(ortho, product)
         ]
+    copies = []
     for head in range(heads):
         out_ref[head] = jnp.transpose(scale * ortho[head].astype(jnp.float32)).astype(jnp.bfloat16)
+        copies.append(pltpu.make_async_copy(out_ref.at[head], out_hbm.at[head], sent.at[head]))
+        copies[head].start()
+    for copy in copies:
+        copy.wait()
 
 
 def body(latent, value_grad, lengths):
@@ -149,7 +154,15 @@
     parts = exchange(blocks, wide)
     parts = exchange(run_kernel(total_kernel, (others, *block), [VMEM], parts), narrow)
     sums = exchange(run_kernel(total_kernel, (members, *block), [VMEM], parts), wide)
-    return run_kernel(ortho_kernel, (heads, KV_RANK, V_DIM), [VMEM], sums)
+    shape = (heads, KV_RANK, V_DIM)
+    return pl.pallas_call(
+        ortho_kernel,
+        out_shape=jax.ShapeDtypeStruct(shape, jnp.bfloat16),
+        in_specs=[VMEM],
+        out_specs=pl.BlockSpec(memory_space=pl.ANY),
+        scratch_shapes=[pltpu.VMEM(shape, jnp.bfloat16), pltpu.SemaphoreType.DMA((heads,))],
+        compiler_params=pltpu.CompilerParams(vmem_limit_bytes=32 * 2**20),
+    )(sums)
 
 
 def solution(mesh):

time: 90.8 us -> 90.7 us (level)
    pallas_call x5 -> x4, Pallas kernels: 5.47 us -> 1.79 us  [run_kernel(): pl.pallas_call(kernel, out_shape=jax.ShapeDtypeStruct(shape, jnp.bfloat16...]
    pallas_call x0 -> x1, Pallas kernels: none -> 3.59 us  [body(): pl.pallas_call(ortho_kernel, out_shape=jax.ShapeDtypeStruct(shape, jnp.bf...]
where the time goes in v5:
time: 90.7 us; the launch traced here: 90.4 us
  blocking collectives  82 us (90%)
  Pallas kernels  5.38 us (6%)
  local copies, waits for them, and re-layouts  2.73 us (3%)
    all_to_all x3, blocking collectives, exchange(): lax.all_to_all(blocks, AXES, 0, 0, axis_index_groups=groups, tiled=True)  60.3 us
    all_gather x1, blocking collectives, body(): lax.all_gather(coded.astype(jnp.float16), ('x', 'c'), axis=0, tiled=True)  21.7 us
    pallas_call x1, Pallas kernels, body(): pl.pallas_call(ortho_kernel, out_shape=jax.ShapeDtypeStruct(shape, jnp.bf...  3.59 us
    unnamed x6, local copies, waits for them, and re-layouts  2.73 us

profile of v5, /device:TPU:32, one launch (start us, length us, event | category | flops | bytes accessed | tf_op | source)
XLA Modules:
  0.0 90.4 jit_solution(8795688259236602135)
XLA Ops:
  0.0 0.0 copy-start.1
  0.0 0.9 copy-done.1
  0.9 0.0 copy-start.2
  0.9 0.7 copy-done.2
  1.5 0.7 shard_map.37
  2.3 21.7 %all-gather.1 = f16[512,1664]{1,0:T(8,128)(2,1)S(1)} all-gather(f16[32,1664]{1,0:T(8,128)(2,1)S(1)} %convert_element_type.6), channel_id=1, replica_groups=mesh['z'=8,'y'=8,'x'=8,'c'=2] {'x','c'}, dimensions={0}, use_global_device_ids=true | all-gather | bytes 1810432 | tf_op jit(solution)/shard_map/all_gather | solution.py:144
  23.9 0.0 copy-start
  23.9 0.2 convert_element_type.7.latent_ref
  24.2 1.2 %copy-done = bf16[1536,512]{1,0:T(8,128)(2,1)S(1)} copy-done((bf16[1536,512]{1,0:T(8,128)(2,1)S(1)}, bf16[1536,512]{1,0:T(8,128)(2,1)}, u32[]{:S(2)}) %copy-start) | copy-done | bytes 1572888
  25.4 1.0 %shard_map.38 = bf16[8,256,128]{2,1,0:T(8,128)(2,1)S(1)} custom-call(bf16[512,1664]{1,0:T(8,128)(2,1)S(1)} %convert_element_type.7.latent_ref, bf16[1536,512]{1,0:T(8,128)(2,1)S(1)} %copy-done), custom_call_target="tpu_custom_call" | custom-call | tf_op jit(solution)/shard_map/pallas_call | solution.py:55
  26.3 24.7 %all_to_all.15.parts_ref = bf16[8,256,128]{2,1,0:T(8,128)(2,1)S(1)} all-to-all(bf16[8,256,128]{2,1,0:T(8,128)(2,1)S(1)} %shard_map.38), channel_id=1, replica_groups={{0,64,48,112,16,80,32,96},{128,192,176,240,144,208,160,224},{256,320,30..., dimensions={0} | all-to-all | bytes 1048576 | tf_op jit(solution)/shard_map/all_to_all | solution.py:51
  51.0 0.1 shard_map.39
  51.1 20.7 %all_to_all.16.parts_ref = bf16[8,256,128]{2,1,0:T(8,128)(2,1)S(1)} all-to-all(bf16[8,256,128]{2,1,0:T(8,128)(2,1)S(1)} %shard_map.39), channel_id=1, replica_groups={{0,512,384,896,128,640,256,768},{16,528,400,912,144,656,272,784},{32,54..., dimensions={0} | all-to-all | bytes 1048576 | tf_op jit(solution)/shard_map/all_to_all | solution.py:51
  71.8 0.1 shard_map.40
  71.8 15.0 %all_to_all.17.sums_ref = bf16[8,256,128]{2,1,0:T(8,128)(2,1)S(1)} all-to-all(bf16[8,256,128]{2,1,0:T(8,128)(2,1)S(1)} %shard_map.40), channel_id=1, replica_groups={{0,64,48,112,16,80,32,96},{128,192,176,240,144,208,160,224},{256,320,30..., dimensions={0} | all-to-all | bytes 1048576 | tf_op jit(solution)/shard_map/all_to_all | solution.py:51
  86.8 3.6 %shard_map.41 = bf16[4,512,128]{2,1,0:T(8,128)(2,1)} custom-call(bf16[8,256,128]{2,1,0:T(8,128)(2,1)S(1)} %all_to_all.17.sums_ref), custom_call_target="tpu_custom_call" | custom-call | tf_op jit(solution)/shard_map/pallas_call | solution.py:158
  (1 shorter events, 0.0 us)
Async XLA Ops:
  0.0 0.9 copy-start.1
  0.9 0.7 copy-start.2
  23.9 1.4 %copy-start = (bf16[1536,512]{1,0:T(8,128)(2,1)S(1)}, bf16[1536,512]{1,0:T(8,128)(2,1)}, u32[]{:S(2)}) copy-start(bf16[1536,512]{1,0:T(8,128)(2,1)} %grad_ref.1) | copy-start | bytes 4718596

commit v6 on v4

--- a/solution.py
+++ b/solution.py
@@ -28,23 +28,19 @@
 SMEM = pl.BlockSpec(memory_space=pltpu.SMEM)
 
 
-ORDER = [0, 4, 3, 7, 1, 5, 2, 6]
-PAIR = 1
+SCATTER = [0, 4, 3, 7, 1, 5, 2, 6]
+ACROSS = [0, 4, 3, 5, 2, 6, 1, 7]
+GATHER = [0, 4, 3, 7, 1, 5, 2, 6]
 
 
-def stage_groups():
+def ring_groups(first, order):
     index = np.arange(np.prod(SIDES)).reshape(SIDES)
-    wide, narrow = [], []
+    rings = []
     for core in range(2):
-        plane = index[..., core] if core == 0 else index[..., core].swapaxes(0, 1)
-        for column in range(SIDES[2]):
-            for start in range(0, SIDES[0], PAIR):
-                ring = plane[start : start + PAIR, ORDER, column]
-                wide.append(ring.reshape(-1).tolist())
-            for place in range(SIDES[1]):
-                for start in range(PAIR):
-                    narrow.append(plane[start::PAIR, place, column][ORDER].tolist())
-    return wide, narrow
+        axis = 1 - core if first else core
+        lines = np.moveaxis(index[..., core], axis, -1).reshape(-1, SIDES[axis])
+        rings += lines[:, order].tolist()
+    return rings
 
 
 def exchange(blocks, groups):
@@ -96,9 +92,10 @@
 def ortho_kernel(sums_ref, out_ref):
     heads = out_ref.shape[0]
     parts = sums_ref.shape[0] // heads
+    place = [GATHER.index(device) for device in SCATTER]
     scale = 0.2 * max(KV_RANK, V_DIM) ** 0.5
     sums = [
-        jnp.concatenate([sums_ref[part * heads + head] for part in range(parts)], axis=0)
+        jnp.concatenate([sums_ref[place[part * heads + head]] for part in range(parts)], axis=0)
         for head in range(heads)
     ]
     turned = [jnp.transpose(g) for g in sums]
@@ -133,11 +130,13 @@
 def body(latent, value_grad, lengths):
     capacity, columns = latent.shape
     heads = value_grad.shape[1] // V_DIM
-    wide, narrow = stage_groups()
+    scatter = ring_groups(True, SCATTER)
+    across = ring_groups(False, ACROSS)
+    gather = ring_groups(True, GATHER)
 
     coded = run_kernel(encode_kernel, (columns, capacity + LANES), [SMEM, VMEM], lengths, latent.T)
     gathered = lax.all_gather(coded.astype(jnp.float16), ("x", "c"), axis=0, tiled=True)
-    members, others = len(wide[0]), len(narrow[0])
+    members = len(SCATTER)
     block = (KV_RANK * heads // members, V_DIM)
     blocks = run_kernel(
         partial_kernel,
@@ -146,9 +145,9 @@
         gathered.astype(jnp.bfloat16),
         value_grad,
     )
-    parts = exchange(blocks, wide)
-    parts = exchange(run_kernel(total_kernel, (others, *block), [VMEM], parts), narrow)
-    sums = exchange(run_kernel(total_kernel, (members, *block), [VMEM], parts), wide)
+    parts = exchange(blocks, scatter)
+    parts = exchange(run_kernel(total_kernel, parts.shape, [VMEM], parts), across)
+    sums = exchange(run_kernel(total_kernel, parts.shape, [VMEM], parts), gather)
     return run_kernel(ortho_kernel, (heads, KV_RANK, V_DIM), [VMEM], sums)
 
 

time: 90.8 us -> 90.6 us (level)
  no operation moved by 1% of the time
where the time goes in v6:
time: 90.6 us; the launch traced here: 90.3 us
  blocking collectives  81.9 us (90%)
  Pallas kernels  5.47 us (6%)
  local copies, waits for them, and re-layouts  2.73 us (3%)
    all_to_all x3, blocking collectives, exchange(): lax.all_to_all(blocks, AXES, 0, 0, axis_index_groups=groups, tiled=True)  60.2 us
    all_gather x1, blocking collectives, body(): lax.all_gather(coded.astype(jnp.float16), ('x', 'c'), axis=0, tiled=True)  21.7 us
    pallas_call x5, Pallas kernels, run_kernel(): pl.pallas_call(kernel, out_shape=jax.ShapeDtypeStruct(shape, jnp.bfloat16...  5.47 us
    unnamed x6, local copies, waits for them, and re-layouts  2.73 us

profile of v6, /device:TPU:32, one launch (start us, length us, event | category | flops | bytes accessed | tf_op | source)
XLA Modules:
  0.0 90.3 jit_solution(9448020620720818746)
XLA Ops:
  0.0 0.0 copy-start.1
  0.0 0.9 copy-done.1
  0.9 0.0 copy-start.2
  0.9 0.7 copy-done.2
  1.5 0.7 shard_map.37
  2.3 21.7 %all-gather.1 = f16[512,1664]{1,0:T(8,128)(2,1)S(1)} all-gather(f16[32,1664]{1,0:T(8,128)(2,1)S(1)} %convert_element_type.6), channel_id=1, replica_groups=mesh['z'=8,'y'=8,'x'=8,'c'=2] {'x','c'}, dimensions={0}, use_global_device_ids=true | all-gather | bytes 1810432 | tf_op jit(solution)/shard_map/all_gather | solution.py:138
  23.9 0.0 copy-start
  23.9 0.2 convert_element_type.7.latent_ref
  24.2 1.2 %copy-done = bf16[1536,512]{1,0:T(8,128)(2,1)S(1)} copy-done((bf16[1536,512]{1,0:T(8,128)(2,1)S(1)}, bf16[1536,512]{1,0:T(8,128)(2,1)}, u32[]{:S(2)}) %copy-start) | copy-done | bytes 1572888
  25.4 1.0 %shard_map.38 = bf16[8,256,128]{2,1,0:T(8,128)(2,1)S(1)} custom-call(bf16[512,1664]{1,0:T(8,128)(2,1)S(1)} %convert_element_type.7.latent_ref, bf16[1536,512]{1,0:T(8,128)(2,1)S(1)} %copy-done), custom_call_target="tpu_custom_call" | custom-call | tf_op jit(solution)/shard_map/pallas_call | solution.py:51
  26.3 24.7 %all_to_all.15.parts_ref = bf16[8,256,128]{2,1,0:T(8,128)(2,1)S(1)} all-to-all(bf16[8,256,128]{2,1,0:T(8,128)(2,1)S(1)} %shard_map.38), channel_id=1, replica_groups={{0,64,48,112,16,80,32,96},{2,66,50,114,18,82,34,98},{4,68,52,116,20,84,..., dimensions={0} | all-to-all | bytes 1048576 | tf_op jit(solution)/shard_map/all_to_all | solution.py:47
  51.0 0.1 shard_map.39
  51.1 20.5 %all_to_all.16.parts_ref = bf16[8,256,128]{2,1,0:T(8,128)(2,1)S(1)} all-to-all(bf16[8,256,128]{2,1,0:T(8,128)(2,1)S(1)} %shard_map.39), channel_id=1, replica_groups={{0,512,384,640,256,768,128,896},{2,514,386,642,258,770,130,898},{4,516,..., dimensions={0} | all-to-all | bytes 1048576 | tf_op jit(solution)/shard_map/all_to_all | solution.py:47
  71.6 0.1 shard_map.40
  71.7 15.0 %all_to_all.17.sums_ref = bf16[8,256,128]{2,1,0:T(8,128)(2,1)S(1)} all-to-all(bf16[8,256,128]{2,1,0:T(8,128)(2,1)S(1)} %shard_map.40), channel_id=1, replica_groups={{0,64,48,112,16,80,32,96},{2,66,50,114,18,82,34,98},{4,68,52,116,20,84,..., dimensions={0} | all-to-all | bytes 1048576 | tf_op jit(solution)/shard_map/all_to_all | solution.py:47
  86.7 3.7 %shard_map.41 = bf16[4,512,128]{2,1,0:T(8,128)(2,1)} custom-call(bf16[8,256,128]{2,1,0:T(8,128)(2,1)S(1)} %all_to_all.17.sums_ref), custom_call_target="tpu_custom_call" | custom-call | tf_op jit(solution)/shard_map/pallas_call | solution.py:51
  (1 shorter events, 0.0 us)
Async XLA Ops:
  0.0 0.9 copy-start.1
  0.9 0.7 copy-start.2
  23.9 1.4 %copy-start = (bf16[1536,512]{1,0:T(8,128)(2,1)S(1)}, bf16[1536,512]{1,0:T(8,128)(2,1)}, u32[]{:S(2)}) copy-start(bf16[1536,512]{1,0:T(8,128)(2,1)} %grad_ref.1) | copy-start | bytes 4718596
